TPU v7x, 128 devices: a whole 4x4x4 slice. The times are simulated.
128 devices in a mesh: col: 16 (over x, z), blk: 8 (over y, core).
Axes of the slice: x: 4, y: 4, z: 4, core: 2. Of those that a mesh axis runs over, the one named last changes fastest.
Arguments:
- col_tiles: bfloat16 [2048, 4, 128, 128], P(('col', 'blk')), may hold values from -0.19921875 to 0.19921875
- scales: float32 [2048, 128], P(('col', 'blk')), may hold values from 0.01 to 100
- positions: int32 [2048, 4], P(('col', 'blk')), may hold values from 0 to 7, as said below
- targets: int32 [2048, 1], P(('col', 'blk')), may hold values from 0 to 7; in each aligned block of 16 rows (0 to 15, 16 to 31, ...) at most 4 rows name the same one
- parents: int32 [16, 8], P('col', 'blk'), may hold values from 0 to 15
Outputs:
- leaf_factor: float32 [128, 512, 512], P(('col', 'blk'))
- leaf_panel: float32 [128, 512, 512], P(('col', 'blk'))
- parent_factor: float32 [128, 512, 512], P(('col', 'blk'))
Inputs may be any that keep to these rules, and one draw needn't show every extreme that they name: `positions`: each column tile names 2 distinct tile rows below 4 and then 2 distinct ones at or above it. `targets`: among the rows of one device no value appears more than 4 times.
All inputs are finite; a program needn't handle non-finite values.
Results may differ from a plain program's by a relative error of at most 0.0047.
Values may be sent and summed in bfloat16 or wider, within the bound.
No kernel may reach another device: no remote copies, remote signals or barrier semaphores. Data moves between devices by JAX's collectives and lax.ppermute only.
A program may use at most 128 MiB of HBM per device.

v0:
```python
import jax
import jax.numpy as jnp
from jax import lax
from jax.sharding import PartitionSpec as P

SUPER = 512


RIDGE = 1.0


def factor_front(front_block):
    identity_mat = jnp.eye(SUPER, dtype=jnp.float32)
    factor = jnp.linalg.cholesky(front_block[:SUPER, :SUPER] + RIDGE * identity_mat)
    leaf_panel = lax.linalg.triangular_solve(
        factor, front_block[SUPER:, :SUPER], left_side=False, lower=True, transpose_a=True
    )
    product = jnp.dot(
        leaf_panel,
        leaf_panel.T,
        precision=lax.Precision.HIGHEST,
        preferred_element_type=jnp.float32,
    )
    return (factor, leaf_panel, front_block[SUPER:, SUPER:] - product)


def on_device(col_tiles, scales, positions, targets, parents):
    tile_count = col_tiles.shape[0]
    pieces = col_tiles.shape[1]
    tile_width = col_tiles.shape[2]
    groups = lax.axis_size("blk")
    capacity = 2 * tile_count // groups
    scaled = (col_tiles.astype(jnp.float32) * jnp.sqrt(scales)[:, None, None, :]).astype(
        jnp.bfloat16
    )
    routed = targets[:, 0]
    dest_marks = (routed[:, None] == jnp.arange(groups, dtype=jnp.int32)[None, :]).astype(jnp.int32)
    rank_in_dest = jnp.sum((jnp.cumsum(dest_marks, axis=0) - dest_marks) * dest_marks, axis=1)
    slot_index = routed * capacity + rank_in_dest
    source = (
        jnp.full((groups * capacity,), -1, jnp.int32)
        .at[slot_index]
        .set(jnp.arange(tile_count, dtype=jnp.int32))
    )
    filled = source >= 0
    chosen = jnp.maximum(source, 0)
    outgoing = jnp.where(filled[:, None, None, None], scaled[chosen], jnp.zeros((), jnp.bfloat16))
    outgoing = outgoing.reshape(groups, capacity, pieces, tile_width, tile_width)
    out_spots = (
        jnp.where(filled[:, None], positions[chosen], -1)
        .astype(jnp.bfloat16)
        .reshape(groups, capacity, pieces)
    )
    incoming, in_spots = (
        lax.all_to_all(outgoing, "blk", split_axis=0, concat_axis=0, tiled=True),
        lax.all_to_all(out_spots, "blk", split_axis=0, concat_axis=0, tiled=True),
    )
    slot_total = groups * capacity
    flat_tiles = incoming.reshape(slot_total, pieces, tile_width, tile_width)
    flat_spots = in_spots.reshape(slot_total, pieces).astype(jnp.int32)
    spot_ids = jnp.arange(2 * (SUPER // tile_width), dtype=jnp.int32)
    onehot = (flat_spots[:, :, None] == spot_ids[None, None, :]).astype(jnp.bfloat16)
    spread_cols = jnp.einsum(
        "kjr,kjac->rakc", onehot, flat_tiles, preferred_element_type=jnp.float32
    ).astype(jnp.bfloat16)
    spread_cols = spread_cols.reshape(2 * SUPER, slot_total * tile_width)
    front_block = lax.dot_general(
        spread_cols, spread_cols, (((1,), (1,)), ((), ())), preferred_element_type=jnp.float32
    )
    leaf_factor, leaf_panel, update = factor_front(front_block)
    my_parent = parents[0, 0]
    row_ids = jnp.arange(lax.axis_size("col") * SUPER, dtype=jnp.int32)
    in_parent = row_ids // SUPER == my_parent
    repeated = jnp.tile(update, (lax.axis_size("col") * SUPER // SUPER, 1))
    summed_block = lax.psum_scatter(
        jnp.where(in_parent[:, None], repeated, jnp.zeros((), jnp.float32)),
        "col",
        scatter_dimension=0,
        tiled=True,
    )
    identity_mat = jnp.eye(SUPER, dtype=jnp.float32)
    parent_factor = jnp.linalg.cholesky(summed_block + RIDGE * identity_mat)
    return (leaf_factor[None], leaf_panel[None], parent_factor[None])


def solution(mesh):
    in_specs = (
        P(("col", "blk"), None, None, None),
        P(("col", "blk"), None),
        P(("col", "blk"), None),
        P(("col", "blk"), None),
        P("col", "blk"),
    )
    out_specs = (
        P(("col", "blk"), None, None),
        P(("col", "blk"), None, None),
        P(("col", "blk"), None, None),
    )
    return jax.shard_map(
        on_device, mesh=mesh, in_specs=in_specs, out_specs=out_specs, check_vma=False
    )
```

profile of v0, /device:TPU:0, one launch (start us, length us, event | category | flops | bytes accessed | tf_op | source)
XLA Modules:
  0.0 504.5 jit_solution(6558996245783400967)
XLA Ops:
  7.2 0.7 fusion.53
  7.9 0.8 select_reduce_fusion.8
  10.1 0.8 copy.41
  11.7 0.7 copy.44
  12.4 4.6 all-to-all-start.1
  17.7 2.2 multiply_convert_fusion
  19.9 3.1 gather_fusion
  23.0 7.5 %copy_select_fusion = bf16[8,4,4,128,128]{4,2,3,1,0:T(4,128)(2,1)} fusion(bf16[8,4,4,128,128]{4,3,2,1,0:T(8,128)(2,1)} %bitcast.109, pred[8,4]{1,0:T(8,128)(4,1)S(1)} %broadcast_in_dim.64), kind=kLoop, calls=%fused_computation.10 | loop fusion | flops 2097152 | bytes 8388640 | tf_op jit(solution)/shard_map/jit(_where)/select_n | solution.py:47
  30.4 4.8 all-to-all-start
  36.4 48.6 %all-to-all-done = bf16[8,4,4,128,128]{4,2,3,1,0:T(4,128)(2,1)} async-done(((bf16[8,4,4,128,128]{4,2,3,1,0:T(4,128)(2,1)}), bf16[8,4,4,128,128]{4,2,3,1,0:T(4,128)(2,1)}, u32[]{:S(2)}, u32[]{:S(2)}) %all-to-all-start) | async-done | bytes 4194336 | tf_op jit(solution)/shard_map/all_to_all | solution.py:55
  85.0 7.9 %convert_bitcast_fusion = bf16[8,128,32,128]{3,0,1,2:T(8,128)(2,1)} fusion(bf16[32,4,128,128]{3,1,2,0:T(4,128)(2,1)} %bitcast.4, s32[32,4]{1,0:T(8,128)S(1)} %bitcast.111), kind=kOutput, calls=%fused_computation.9 | convolution fusion | flops 37749760 | bytes 12583424 | tf_op jit(solution)/shard_map/kjr,kjac->rakc/dot_general | solution.py:63
  92.9 12.0 %copy.48 = bf16[8,128,32,128]{3,2,1,0:T(8,128)(2,1)} copy(bf16[8,128,32,128]{3,0,1,2:T(8,128)(2,1)} %convert_bitcast_fusion) | data formatting | bytes 16777216 | tf_op jit(solution)/shard_map/convert_element_type | solution.py:65
  104.9 14.1 %fusion = f32[1024,1024]{1,0:T(8,128)S(1)} fusion(bf16[128,8,32,128]{3,2,1,0:T(8,128)(2,1)} %bitcast.110), kind=kOutput, calls=%fused_computation.5 | convolution fusion | flops 8589934592 | bytes 12582912 | tf_op jit(solution)/shard_map/dot_general | solution.py:67
  119.0 1.9 copy-done.1
  122.0 11.7 %cholesky.286 = f32[128,128]{1,0:T(8,128)S(1)} custom-call(f32[128,128]{1,0:T(8,128)S(1)} %cholesky.426), custom_call_target="Cholesky" | custom-call | tf_op jit(solution)/shard_map/jit(cholesky)/cholesky | solution.py:14
  133.8 9.8 %custom-call.27 = f32[1,128,128]{1,2,0:T(8,128)S(1)} custom-call(f32[1,128,128]{2,1,0:T(8,128)S(1)} %get-tuple-element.55), custom_call_target="InvertDiagBlocksLowerTriangular" | custom-call | tf_op jit(solution)/shard_map/jit(cholesky)/cholesky | solution.py:14
  144.4 11.7 %cholesky.305 = f32[128,128]{1,0:T(8,128)S(1)} custom-call(f32[128,128]{1,0:T(8,128)S(1)} %cholesky.430), custom_call_target="Cholesky" | custom-call | tf_op jit(solution)/shard_map/jit(cholesky)/cholesky | solution.py:14
  156.1 10.0 %custom-call.28 = f32[1,128,128]{1,2,0:T(8,128)S(1)} custom-call(f32[1,128,128]{2,1,0:T(8,128)S(1)} %get-tuple-element.52), custom_call_target="InvertDiagBlocksLowerTriangular" | custom-call | tf_op jit(solution)/shard_map/jit(cholesky)/cholesky | solution.py:14
  166.8 11.7 %cholesky.326 = f32[128,128]{1,0:T(8,128)S(1)} custom-call(f32[128,128]{1,0:T(8,128)S(1)} %cholesky.435), custom_call_target="Cholesky" | custom-call | tf_op jit(solution)/shard_map/jit(cholesky)/cholesky | solution.py:14
  179.2 9.8 %custom-call.29 = f32[1,128,128]{1,2,0:T(8,128)S(1)} custom-call(f32[1,128,128]{2,1,0:T(8,128)S(1)} %get-tuple-element.49), custom_call_target="InvertDiagBlocksLowerTriangular" | custom-call | tf_op jit(solution)/shard_map/jit(cholesky)/cholesky | solution.py:14
  189.6 12.1 %cholesky.343 = f32[128,128]{1,0:T(8,128)S(1)} custom-call(f32[128,128]{1,0:T(8,128)S(1)} %convolution_subtract_fusion.9), custom_call_target="Cholesky" | custom-call | tf_op jit(solution)/shard_map/jit(cholesky)/cholesky | solution.py:14
  205.6 1.2 fusion.5
  206.8 7.9 %while.1 = (s32[]{:T(128)}, f32[512,512]{1,0:T(8,128)S(1)}, s32[4,2]{0,1:T(2,128)S(1)}, f32[4,128,128]{2,1,0:T(8,128)S(1)}, s32[]{:T(128)}) while((s32[]{:T(128)}, f32[512,512]{1,0:T(8,128)S(1)}, s32[4,2]{0,1:T(2,128)S(1)}, f32[4,128,128]{2,1,0:T(8,128)S(1)}, s32[]{:T(128)}) %tuple.44), condition=%wide.while_cond, body=%wide.while_body.sunk | while | flops 2 | bytes 131189 | solution.py:15
  207.4 1.4 bitcast_dynamic-update-slice_fusion.2
  209.4 1.4 bitcast_dynamic-update-slice_fusion.2
  211.3 1.4 bitcast_dynamic-update-slice_fusion.2
  213.3 1.4 bitcast_dynamic-update-slice_fusion.2
  214.7 39.3 %custom-call.23 = f32[4,128,128]{1,2,0:T(8,128)S(1)} custom-call(f32[4,128,128]{2,1,0:T(8,128)S(1)} %get-tuple-element.11), custom_call_target="InvertDiagBlocksLowerTriangular" | custom-call | tf_op jit(solution)/shard_map/triangular_solve | solution.py:15
  254.0 1.4 fusion.17
  255.4 1.5 convolution_subtract_fusion.2
  257.3 1.9 convolution_subtract_fusion.1
  259.7 2.4 convolution_subtract_fusion.3
  262.6 3.1 convolution_subtract_fusion
  266.0 7.9 %tile.4 = f32[16,512,512]{1,0,2:T(8,128)} broadcast(f32[512,512]{0,1:T(8,128)S(1)} %copy.51), dimensions={1,2} | broadcast | bytes 17825792 | tf_op jit(solution)/shard_map/tile | solution.py:74
  273.9 19.1 %copy.61 = f32[64,8,16,512]{3,1,2,0:T(8,128)S(1)} copy(f32[64,8,16,512]{3,2,1,0:T(8,128)} %bitcast.108) | data formatting | bytes 33554432
  293.0 6.2 %broadcast_select_fusion = f32[8192,512]{0,1:T(8,128)} fusion(f32[8192,512]{0,1:T(8,128)S(1)} %bitcast.107, pred[8192]{0:T(1024)(128)(4,1)S(1)} %fusion.48), kind=kLoop, calls=%fused_computation.8 | loop fusion | flops 4194304 | bytes 33562624 | tf_op jit(solution)/shard_map/jit(_where)/select_n | solution.py:76
  299.3 1.3 copy.53
  300.6 109.9 %reduce-scatter.2.cloned.1.call-done = f32[512,512]{0,1:T(8,128)} async-done(((f32[8192,512]{0,1:T(8,128)}), f32[512,512]{0,1:T(8,128)}) %reduce-scatter.2.cloned.1.call-update) | async-done | bytes 1048592 | tf_op jit(solution)/shard_map/reduce_scatter | solution.py:75
  410.5 1.4 convert_add_fusion
  412.5 11.7 %cholesky.358 = f32[128,128]{1,0:T(8,128)S(1)} custom-call(f32[128,128]{1,0:T(8,128)S(1)} %cholesky.439), custom_call_target="Cholesky" | custom-call | tf_op jit(solution)/shard_map/jit(cholesky)/cholesky | solution.py:82
  425.0 9.8 %custom-call.30 = f32[1,128,128]{1,2,0:T(8,128)S(1)} custom-call(f32[1,128,128]{2,1,0:T(8,128)S(1)} %get-tuple-element.45), custom_call_target="InvertDiagBlocksLowerTriangular" | custom-call | tf_op jit(solution)/shard_map/jit(cholesky)/cholesky | solution.py:82
  435.5 11.7 %cholesky.377 = f32[128,128]{1,0:T(8,128)S(1)} custom-call(f32[128,128]{1,0:T(8,128)S(1)} %cholesky.443), custom_call_target="Cholesky" | custom-call | tf_op jit(solution)/shard_map/jit(cholesky)/cholesky | solution.py:82
  447.2 0.7 compare_reduce_fusion.2
  448.0 10.0 %custom-call.31 = f32[1,128,128]{1,2,0:T(8,128)S(1)} custom-call(f32[1,128,128]{2,1,0:T(8,128)S(1)} %get-tuple-element.42), custom_call_target="InvertDiagBlocksLowerTriangular" | custom-call | tf_op jit(solution)/shard_map/jit(cholesky)/cholesky | solution.py:82
  458.6 11.7 %cholesky.398 = f32[128,128]{1,0:T(8,128)S(1)} custom-call(f32[128,128]{1,0:T(8,128)S(1)} %cholesky.448), custom_call_target="Cholesky" | custom-call | tf_op jit(solution)/shard_map/jit(cholesky)/cholesky | solution.py:82
  471.0 9.8 %custom-call.32 = f32[1,128,128]{1,2,0:T(8,128)S(1)} custom-call(f32[1,128,128]{2,1,0:T(8,128)S(1)} %get-tuple-element.39), custom_call_target="InvertDiagBlocksLowerTriangular" | custom-call | tf_op jit(solution)/shard_map/jit(cholesky)/cholesky | solution.py:82
  481.4 11.7 %cholesky.415 = f32[128,128]{1,0:T(8,128)S(1)} custom-call(f32[128,128]{1,0:T(8,128)S(1)} %convolution_subtract_fusion.8), custom_call_target="Cholesky" | custom-call | tf_op jit(solution)/shard_map/jit(cholesky)/cholesky | solution.py:82
  496.4 1.1 select_bitcast_fusion
  (80 shorter events, 17.3 us)
Async XLA Ops:
  12.4 18.0 %all-to-all-start.1 = ((bf16[8,4,4]{1,2,0:T(4,128)(2,1)}), bf16[8,4,4]{1,2,0:T(4,128)(2,1)S(1)}, u32[]{:S(2)}, u32[]{:S(2)}) async-start(bf16[8,4,4]{1,2,0:T(4,128)(2,1)} %copy.44), calls=%async_computation.1 | async-start | bytes 16384 | tf_op jit(solution)/shard_map/all_to_all | solution.py:56
  30.4 54.6 %all-to-all-start = ((bf16[8,4,4,128,128]{4,2,3,1,0:T(4,128)(2,1)}), bf16[8,4,4,128,128]{4,2,3,1,0:T(4,128)(2,1)}, u32[]{:S(2)}, u32[]{:S(2)}) async-start(bf16[8,4,4,128,128]{4,2,3,1,0:T(4,128)(2,1)} %copy_select_fusion), calls=%async_computation | async-start | bytes 8388608 | tf_op jit(solution)/shard_map/all_to_all | solution.py:55
  35.2 375.2 %reduce-scatter.2.cloned.1.call-start = ((), (), s32[]{:S(2)}) async-start(), calls=%async_computation.3 | async-start | bytes 17825792 | tf_op jit(solution)/shard_map/reduce_scatter | solution.py:75
  119.0 1.9 copy-start.1
  410.5 1.8 copy-start
Sparse Core Ops, SparseCore 0:
  299.3 111.1 reduce-scatter.1
where the time goes:
time: 510 us; the launch traced here: 505 us
  other arithmetic  220 us (43%)
  waiting for transfers between devices  159 us (31%)
  local copies, waits for them, and re-layouts  58.6 us (11%)
  matrix products  37.3 us (7%)
  between operations  20.4 us (4%)
  starting transfers between devices  9.57 us (2%)
    reduce_scatter x1, waiting for transfers between devices, on_device(): lax.psum_scatter(jnp.where(in_parent[:, None], repeated, jnp.zeros((), jn...  110 us
    another operation x15, other arithmetic, on_device(): parent_factor = jnp.linalg.cholesky(summed_block + RIDGE * identity_mat)  79.3 us
    another operation x14, other arithmetic, factor_front(): jnp.linalg.cholesky(front_block[:SUPER, :SUPER] + RIDGE * identity_mat)  78.9 us
    all_to_all x1, waiting for transfers between devices, on_device(): lax.all_to_all(outgoing, 'blk', split_axis=0, concat_axis=0, tiled=True)  48.6 us
    another operation x3, other arithmetic, factor_front(): lax.linalg.triangular_solve(factor, front_block[SUPER:, :SUPER], left_sid...  40.6 us
    unnamed x8, local copies, waits for them, and re-layouts  23.4 us
    dot_general x1, matrix products, on_device(): lax.dot_general(spread_cols, spread_cols, (((1,), (1,)), ((), ())), prefe...  14.1 us
    convert_element_type x1, local copies, waits for them, and re-layouts, on_device(): spread_cols = jnp.einsum('kjr,kjac->rakc', onehot, flat_tiles, preferred_...  12 us
  transfers between devices with their start and end apart: 3, of which 2 were waited for; matrix products, arithmetic and copies ran while one was open for 3% of the time, Pallas kernels for 0%

commit v1 on v0

v1 whole, which is shorter than its diff:
```python
import functools

import jax
import jax.numpy as jnp
from jax import lax
from jax.experimental import pallas as pl
from jax.experimental.pallas import tpu as pltpu
from jax.sharding import PartitionSpec as P

TILE = 128
SUPER = 512
RIDGE = 1.0
N_BLK = 8
CAP = 4
CT_DEV = 16
RING = 4
META = 5 * CT_DEV
GROUP = 8
LOWER = [(i, j) for j in range(4) for i in range(j, 4)]

F32 = jnp.float32
BF16 = jnp.bfloat16
NT = (((1,), (1,)), ((), ()))
NN = (((1,), (0,)), ((), ()))

VMEM = pl.BlockSpec(memory_space=pltpu.VMEM)
SMEM = pl.BlockSpec(memory_space=pltpu.SMEM)
PARAMS = pltpu.CompilerParams(vmem_limit_bytes=56 << 20)


def split(a):
    high = a.astype(BF16)
    return high, (a - high.astype(F32)).astype(BF16)


def dot3(a, b, dims=NT):
    def one(x, y):
        return lax.dot_general(x, y, dims, preferred_element_type=F32)

    return one(a[0], b[0]) + (one(a[0], b[1]) + one(a[1], b[0]))


def rows_of(pair, start, stop=None):
    return tuple(part[start:stop] for part in pair)


def place_kernel(target_ref, scale_ref, tile_ref, out_ref, count_ref):
    for group in range(N_BLK):
        count_ref[group] = 0

    def one(t, carry):
        owner = target_ref[t, 0]
        rank = count_ref[owner]
        count_ref[owner] = rank + 1
        root = jnp.sqrt(scale_ref[pl.ds(t, 1), :])
        for k in range(2):
            scaled = tile_ref[t, k].astype(F32) * root
            out_ref[owner, rank, k] = scaled.astype(BF16)
        return carry

    lax.fori_loop(0, CT_DEV, one, 0)


def place(col_tiles, scales, targets, half):
    return pl.pallas_call(
        place_kernel,
        grid=(1,),
        in_specs=[
            SMEM,
            pl.BlockSpec((CT_DEV, TILE), lambda i: (0, 0)),
            pl.BlockSpec((CT_DEV, 2, TILE, TILE), lambda i: (0, half, 0, 0)),
        ],
        out_specs=pl.BlockSpec((N_BLK, CAP, 2, TILE, TILE), lambda i: (0, 0, 0, 0, 0)),
        out_shape=jax.ShapeDtypeStruct((N_BLK, CAP, 2, TILE, TILE), BF16),
        scratch_shapes=[pltpu.SMEM((N_BLK,), jnp.int32)],
        compiler_params=PARAMS,
        name=f"place{half}",
    )(targets, scales, col_tiles)


def list_slots(meta_ref, slot_ref):
    me = lax.axis_index("blk")

    def device(b, total):
        def tile(t, carry):
            total, rank = carry
            mine = meta_ref[b * META + 4 * CT_DEV + t] == me

            @pl.when(mine)
            def _():
                slot_ref[5 * total] = b * CAP + rank
                for k in range(4):
                    slot_ref[5 * total + 1 + k] = meta_ref[b * META + 4 * t + k]

            step = mine.astype(jnp.int32)
            return total + step, rank + step

        return lax.fori_loop(0, CT_DEV, tile, (total, 0))[0]

    return lax.fori_loop(0, N_BLK, device, 0)


def spread(in_ref, slot_ref, s_ref, group, total, half):
    s_ref[...] = jnp.zeros(s_ref.shape, BF16)

    def one(i, carry):
        n = group * GROUP + i
        slot = slot_ref[5 * n]
        at = pl.multiple_of(i * TILE, TILE)
        for k in range(2):
            row = slot_ref[5 * n + 1 + 2 * half + k] - 4 * half
            row = pl.multiple_of(row * TILE, TILE)
            s_ref[pl.ds(row, TILE), pl.ds(at, TILE)] = in_ref[slot // CAP, slot % CAP, k]
        return carry

    lax.fori_loop(0, jnp.minimum(GROUP, total - group * GROUP), one, 0)


def add_gram(m_ref, s_ref):
    for j in range(2):
        o = 256 * j
        got = lax.dot_general(s_ref[o:, :], s_ref[o : o + 256, :], NT, preferred_element_type=F32)
        m_ref[2 * j, o:, :] += got[:, :TILE]
        m_ref[2 * j + 1, o:, :] += got[:, TILE:]


def lane(v, j):
    return jnp.broadcast_to(v[:, j : j + 1], (8, TILE))


def sub(v, i):
    return jnp.broadcast_to(v[i : i + 1, :], (8, TILE))


def eliminate64(aug):
    w = [aug[8 * q : 8 * q + 8] for q in range(8)]
    out = []
    sid = lax.broadcasted_iota(jnp.int32, (8, TILE), 0)
    for p in range(8):
        cols = [[lane(w[q], 8 * p + k) for k in range(8)] for q in range(p, 8)]
        rows = [sub(w[p], k) for k in range(8)]
        own = cols[0]
        for k in range(8):
            r = lax.rsqrt(sub(own[k], k))
            low = own[k] * r
            mult = [None] * 8
            for i in range(k + 1, 8):
                mult[i] = sub(low, i)
            for j in range(k + 1, 8):
                own[j] = own[j] - low * mult[j]
            rows[k] = rows[k] * r
            for i in range(k + 1, 8):
                rows[i] = rows[i] - mult[i] * rows[k]
            for q in range(p + 1, 8):
                col = cols[q - p]
                lq = col[k] * r
                for j in range(k + 1, 8):
                    col[j] = col[j] - lq * mult[j]
                w[q] = w[q] - lq * rows[k]
        block = rows[0]
        for k in range(1, 8):
            block = jnp.where(sid == k, rows[k], block)
        out.append(block)
    return jnp.concatenate(out, axis=0)


def factor(m_ref, l_ref, x_ref=None):
    col_id = lax.broadcasted_iota(jnp.int32, (64, TILE), 1)
    row_id = lax.broadcasted_iota(jnp.int32, (64, TILE), 0)
    eye = (col_id == row_id + 64).astype(F32)
    left = col_id < 64
    lower = row_id[:, :64] >= col_id[:, :64]
    zero = jnp.zeros((64, 64), F32)
    for kb in range(4):
        o = TILE * kb
        if kb:
            l_ref[:o, o : o + TILE] = jnp.zeros((o, TILE), F32)
        w1 = eliminate64(jnp.where(left, m_ref[kb, o : o + 64, :], eye))
        x1 = pltpu.roll(w1, 64, 1)[:, :64]
        x1s = split(x1)
        below = m_ref[kb, o + 64 : o + TILE, :]
        l21 = dot3(split(below[:, :64]), x1s)
        l21s = split(l21)
        rest = pltpu.roll(below, 64, 1)[:, :64] - dot3(l21s, l21s)
        w2 = eliminate64(jnp.where(left, jnp.concatenate([rest, rest], axis=1), eye))
        x2 = pltpu.roll(w2, 64, 1)[:, :64]
        x21 = -dot3(split(x2), split(dot3(l21s, x1s, NN)), NN)
        x = jnp.concatenate(
            [jnp.concatenate([x1, zero], axis=1), jnp.concatenate([x21, x2], axis=1)], axis=0
        )
        if x_ref is not None:
            x_ref[kb] = x
        l1 = jnp.where(lower, w1[:, :64].T, 0.0)
        l2 = jnp.where(lower, w2[:, :64].T, 0.0)
        l_ref[o : o + TILE, o : o + TILE] = jnp.concatenate(
            [jnp.concatenate([l1, zero], axis=1), jnp.concatenate([l21, l2], axis=1)], axis=0
        )
        if kb < 3:
            panel = dot3(split(m_ref[kb, o + TILE :, :]), split(x))
            l_ref[o + TILE :, o : o + TILE] = panel
            panels = split(panel)
            for j in range(kb + 1, 4):
                s = TILE * (j - kb - 1)
                m_ref[j, TILE * j :, :] -= dot3(rows_of(panels, s), rows_of(panels, s, s + TILE))


def add_ridge(m_ref):
    row = lax.broadcasted_iota(jnp.int32, (TILE, TILE), 0)
    col = lax.broadcasted_iota(jnp.int32, (TILE, TILE), 1)
    ridge = jnp.where(row == col, jnp.float32(RIDGE), 0.0)
    for j in range(4):
        m_ref[j, TILE * j : TILE * (j + 1), :] += ridge


def leaf_kernel(meta_ref, in_ref, l_ref, x_ref, m_ref, s_ref, slot_ref):
    total = list_slots(meta_ref, slot_ref)
    m_ref[...] = jnp.zeros(m_ref.shape, F32)

    def step(group, carry):
        spread(in_ref, slot_ref, s_ref, group, total, 0)
        add_gram(m_ref, s_ref)
        return carry

    lax.fori_loop(0, (total + GROUP - 1) // GROUP, step, 0)
    add_ridge(m_ref)
    factor(m_ref, l_ref, x_ref)


def leaf(meta, incoming):
    return pl.pallas_call(
        leaf_kernel,
        in_specs=[SMEM, VMEM],
        out_specs=[VMEM, VMEM],
        out_shape=[
            jax.ShapeDtypeStruct((SUPER, SUPER), F32),
            jax.ShapeDtypeStruct((4, TILE, TILE), F32),
        ],
        scratch_shapes=[
            pltpu.VMEM((4, SUPER, TILE), F32),
            pltpu.VMEM((SUPER, GROUP * TILE), BF16),
            pltpu.SMEM((5 * N_BLK * CAP,), jnp.int32),
        ],
        compiler_params=PARAMS,
        name="leaf",
    )(meta, incoming)


def panel_kernel(
    meta_ref, in1_ref, in2_ref, l_ref, x_ref, p_ref, u_ref, f_ref, m_ref, s1_ref, s2_ref, slot_ref
):
    total = list_slots(meta_ref, slot_ref)
    m_ref[...] = jnp.zeros(m_ref.shape, F32)
    f_ref[...] = jnp.zeros(f_ref.shape, F32)

    def step(group, carry):
        spread(in1_ref, slot_ref, s1_ref, group, total, 0)
        spread(in2_ref, slot_ref, s2_ref, group, total, 1)
        f_ref[...] += lax.dot_general(s2_ref[...], s1_ref[...], NT, preferred_element_type=F32)
        add_gram(m_ref, s2_ref)
        return carry

    lax.fori_loop(0, (total + GROUP - 1) // GROUP, step, 0)
    pairs = []
    for kb in range(4):
        o = TILE * kb
        rest = f_ref[:, o : o + TILE]
        for j in range(kb):
            rest = rest - dot3(pairs[j], split(l_ref[o : o + TILE, TILE * j : TILE * (j + 1)]))
        panel = dot3(split(rest), split(x_ref[kb]))
        p_ref[:, o : o + TILE] = panel
        pairs.append(split(panel))
    whole = tuple(jnp.concatenate([pair[i] for pair in pairs], axis=1) for i in range(2))
    n = 0
    for j in range(4):
        o = TILE * j
        update = m_ref[j, o:, :] - dot3(rows_of(whole, o), rows_of(whole, o, o + TILE))
        for i in range(4 - j):
            u_ref[n] = update[TILE * i : TILE * (i + 1)].astype(BF16)
            n += 1


def panel(meta, first, second, leaf_factor, inverses):
    return pl.pallas_call(
        panel_kernel,
        in_specs=[SMEM, VMEM, VMEM, VMEM, VMEM],
        out_specs=[VMEM, VMEM],
        out_shape=[
            jax.ShapeDtypeStruct((SUPER, SUPER), F32),
            jax.ShapeDtypeStruct((len(LOWER), TILE, TILE), BF16),
        ],
        scratch_shapes=[
            pltpu.VMEM((SUPER, SUPER), F32),
            pltpu.VMEM((4, SUPER, TILE), F32),
            pltpu.VMEM((SUPER, GROUP * TILE), BF16),
            pltpu.VMEM((SUPER, GROUP * TILE), BF16),
            pltpu.SMEM((5 * N_BLK * CAP,), jnp.int32),
        ],
        compiler_params=PARAMS,
        name="panel",
    )(meta, first, second, leaf_factor, inverses)


def sort_kernel(parent_ref, a0, a1, a2, a3, keep_ref, b1, b2, b3):
    c = lax.axis_index("col")
    x, z = c // RING, c % RING
    came = (a0, a1, a2, a3)
    owners = [parent_ref[lax.rem(x + RING - s, RING) * RING + z] for s in range(RING)]
    for step, out in enumerate((keep_ref, b1, b2, b3)):
        parent = x * RING + lax.rem(z + step, RING)
        takes = [owner == parent for owner in owners]
        for n in range(len(LOWER)):
            total = jnp.zeros((TILE, TILE), F32)
            for take, ref in zip(takes, came):
                total = total + jnp.where(take, ref[n].astype(F32), 0.0)
            out[n] = total.astype(out.dtype)


def sort(parents, came):
    shape = (len(LOWER), TILE, TILE)
    return pl.pallas_call(
        sort_kernel,
        in_specs=[SMEM] + [VMEM] * 4,
        out_specs=[VMEM] * 4,
        out_shape=[jax.ShapeDtypeStruct(shape, t) for t in (F32, BF16, BF16, BF16)],
        compiler_params=PARAMS,
        name="sort",
    )(parents, *came)


def parent_kernel(keep_ref, b1, b2, b3, l_ref, m_ref):
    for n, (i, j) in enumerate(LOWER):
        got = b1[n].astype(F32) + b2[n].astype(F32) + b3[n].astype(F32)
        m_ref[j, TILE * i : TILE * (i + 1), :] = keep_ref[n] + got
    add_ridge(m_ref)
    factor(m_ref, l_ref)


def parent(parts):
    return pl.pallas_call(
        parent_kernel,
        in_specs=[VMEM] * 4,
        out_specs=VMEM,
        out_shape=jax.ShapeDtypeStruct((SUPER, SUPER), F32),
        scratch_shapes=[pltpu.VMEM((4, SUPER, TILE), F32)],
        compiler_params=PARAMS,
        name="parent",
    )(*parts)


def shift(value, along_x, step):
    pairs = []
    for x in range(RING):
        for z in range(RING):
            to = ((x + step) % RING, z) if along_x else (x, (z + step) % RING)
            pairs.append((x * RING + z, to[0] * RING + to[1]))
    return lax.ppermute(value, "col", pairs)


def on_device(col_tiles, scales, positions, targets, parents):
    meta = jnp.concatenate([positions.reshape(-1), targets.reshape(-1)])
    meta = lax.all_gather(meta, "blk", tiled=True)
    owners = lax.all_gather(parents.reshape(-1), "col", tiled=True)

    def exchange(value):
        return lax.all_to_all(value, "blk", split_axis=0, concat_axis=0, tiled=True)

    out1 = place(col_tiles, scales, targets, 0)
    in1 = exchange(out1)
    out2 = place(col_tiles, scales, targets, 1)
    in1, out2 = lax.optimization_barrier((in1, out2))
    in2 = exchange(out2)
    leaf_factor, inverses = leaf(meta, in1)
    leaf_panel, update = panel(meta, in1, in2, leaf_factor, inverses)
    came = [update] + [shift(update, True, s) for s in (1, 2, 3)]
    keep, *sends = sort(owners, came)
    parts = [keep] + [shift(value, False, s + 1) for s, value in enumerate(sends)]
    parent_factor = parent(parts)
    return (leaf_factor[None], leaf_panel[None], parent_factor[None])


def solution(mesh):
    in_specs = (
        P(("col", "blk"), None, None, None),
        P(("col", "blk"), None),
        P(("col", "blk"), None),
        P(("col", "blk"), None),
        P("col", "blk"),
    )
    out_specs = (
        P(("col", "blk"), None, None),
        P(("col", "blk"), None, None),
        P(("col", "blk"), None, None),
    )
    return jax.shard_map(
        on_device, mesh=mesh, in_specs=in_specs, out_specs=out_specs, check_vma=False
    )
```

time: 510 us -> 175 us (0.34)
  other arithmetic: 220 us -> 0.19 us
  waiting for transfers between devices: 159 us -> 36.1 us
  Pallas kernels: 0 us -> 66.9 us
  local copies, waits for them, and re-layouts: 58.6 us -> 5.95 us
  blocking collectives: 0 us -> 46.2 us
  matrix products: 37.3 us -> 0 us
  between operations: 20.4 us -> 2.06 us
  starting transfers between devices: 9.57 us -> 17 us
    another operation x33 -> x0, other arithmetic: 199 us -> none  [the longest x15 79.3 us: on_device(): parent_factor = jnp.linalg.cholesky(summed_block + RIDGE * identity_mat)]
    reduce_scatter x1 -> x0, waiting for transfers between devices: 110 us -> none  [on_device(): lax.psum_scatter(jnp.where(in_parent[:, None], repeated, jnp.zeros((), jn...]
    pallas_call x0 -> x6, Pallas kernels: none -> 66.9 us  [the longest x1 25.2 us: leaf(): pl.pallas_call(leaf_kernel, in_specs=[SMEM, VMEM], out_specs=[VMEM, VMEM]...]
    unnamed x0 -> x1, blocking collectives: none -> 28.9 us
    dot_general x3 -> x0, matrix products: 25.1 us -> none  [the longest x1 14.1 us: on_device(): lax.dot_general(spread_cols, spread_cols, (((1,), (1,)), ((), ())), prefe...]
    all_to_all x2, waiting for transfers between devices: 48.6 us -> 24.3 us  [exchange(): return lax.all_to_all(value, 'blk', split_axis=0, concat_axis=0, tiled=True)]
    unnamed x8 -> x29, local copies, waits for them, and re-layouts: 23.4 us -> 5.86 us
    all_gather x0 -> x1, blocking collectives: none -> 17.3 us  [on_device(): owners = lax.all_gather(parents.reshape(-1), 'col', tiled=True)]
  transfers between devices with their start and end apart: 3 -> 8, of which waited for: 2 -> 2; matrix products, arithmetic and copies ran while one was open for 3% -> 1% of each run, Pallas kernels for 0% -> 16%
where the time goes in v1:
time: 175 us; the launch traced here: 174 us
  Pallas kernels  66.9 us (38%)
  blocking collectives  46.2 us (26%)
  waiting for transfers between devices  36.1 us (21%)
  starting transfers between devices  17 us (10%)
  local copies, waits for them, and re-layouts  5.95 us (3%)
  between operations  2.06 us (1%)
    unnamed x1, blocking collectives  28.9 us
    pallas_call x1, Pallas kernels, leaf(): pl.pallas_call(leaf_kernel, in_specs=[SMEM, VMEM], out_specs=[VMEM, VMEM]...  25.2 us
    all_to_all x2, waiting for transfers between devices, exchange(): return lax.all_to_all(value, 'blk', split_axis=0, concat_axis=0, tiled=True)  24.3 us
    pallas_call x1, Pallas kernels, parent(): pl.pallas_call(parent_kernel, in_specs=[VMEM] * 4, out_specs=VMEM, out_sh...  20.6 us
    all_gather x1, blocking collectives, on_device(): owners = lax.all_gather(parents.reshape(-1), 'col', tiled=True)  17.3 us
    pallas_call x1, Pallas kernels, panel(): pl.pallas_call(panel_kernel, in_specs=[SMEM, VMEM, VMEM, VMEM, VMEM], out...  12.3 us
    ppermute x6, waiting for transfers between devices, shift(): return lax.ppermute(value, 'col', pairs)  11.8 us
    all_to_all x2, starting transfers between devices, exchange(): return lax.all_to_all(value, 'blk', split_axis=0, concat_axis=0, tiled=True)  8.91 us
  transfers between devices with their start and end apart: 8, of which 2 were waited for; matrix products, arithmetic and copies ran while one was open for 1% of the time, Pallas kernels for 16%

profile of v1, /device:TPU:0, one launch (start us, length us, event | category | flops | bytes accessed | tf_op | source)
XLA Modules:
  0.0 174.4 jit_solution(16281399885254936977)
XLA Ops:
  0.6 1.3 copy.12.target_ref
  2.0 2.9 %place0.1 = bf16[8,4,2,128,128]{4,3,2,1,0:T(8,128)(2,1)} custom-call(s32[16,1]{1,0:T(8,128)} %copy.12.target_ref, f32[16,128]{1,0:T(8,128)} %scale_ref.3, bf16[16,4,128,128]{3,2,1,0:T(8,128)(2,1)} %tile_ref.3), custom_call_target="tpu_custom_call" | custom-call | tf_op jit(solution)/shard_map/place0/pallas_call | solution.py:65
  4.8 4.6 %all-to-all-start = ((bf16[8,4,2,128,128]{4,3,2,1,0:T(8,128)(2,1)}), bf16[8,4,2,128,128]{4,3,2,1,0:T(8,128)(2,1)S(1)}, u32[]{:S(2)}, u32[]{:S(2)}) async-start(bf16[8,4,2,128,128]{4,3,2,1,0:T(8,128)(2,1)} %place0.1), calls=%async_computation | async-start | bytes 4194304 | tf_op jit(solution)/shard_map/all_to_all | solution.py:365
  9.4 2.9 %place1.1 = bf16[8,4,2,128,128]{4,3,2,1,0:T(8,128)(2,1)} custom-call(s32[16,1]{1,0:T(8,128)} %copy.12.target_ref, f32[16,128]{1,0:T(8,128)} %scale_ref.3, bf16[16,4,128,128]{3,2,1,0:T(8,128)(2,1)} %tile_ref.3), custom_call_target="tpu_custom_call" | custom-call | tf_op jit(solution)/shard_map/place1/pallas_call | solution.py:65
  12.3 0.0 copy-start.7
  12.3 0.0 copy-start.10
  12.3 0.0 copy-start.8
  12.3 24.3 %all-to-all-done.in_ref.in1_ref = bf16[8,4,2,128,128]{4,3,2,1,0:T(8,128)(2,1)S(1)} async-done(((bf16[8,4,2,128,128]{4,3,2,1,0:T(8,128)(2,1)}), bf16[8,4,2,128,128]{4,3,2,1,0:T(8,128)(2,1)S(1)}, u32[]{:S(2)}, u32[]{:S(2)}) %all-to-all-start) | async-done | bytes 2097184 | tf_op jit(solution)/shard_map/all_to_all | solution.py:365
  36.6 4.4 %all-to-all-start.1 = ((bf16[8,4,2,128,128]{4,3,2,1,0:T(8,128)(2,1)}), bf16[8,4,2,128,128]{4,3,2,1,0:T(8,128)(2,1)}, u32[]{:S(2)}, u32[]{:S(2)}) async-start(bf16[8,4,2,128,128]{4,3,2,1,0:T(8,128)(2,1)} %place1.1), calls=%async_computation.1 | async-start | bytes 4194304 | tf_op jit(solution)/shard_map/all_to_all | solution.py:365
  41.0 0.0 copy-done
  41.0 0.0 copy-done.7
  41.0 0.1 copy.11
  41.1 0.1 reshape.15
  41.2 0.0 copy-done.10
  41.2 0.6 dynamic-slice
  42.4 0.0 copy-done.8
  42.4 0.2 add_dynamic-update-slice_fusion
  42.6 28.9 %all-reduce.meta_ref = s32[640]{0:T(1024)} all-reduce(s32[640]{0:T(1024)S(1)} %add_dynamic-update-slice_fusion), channel_id=1, replica_groups=mesh['col'=16,'blk'=8] {'blk'}, use_global_device_ids=true, to_apply=%add | all-reduce | flops 640 | bytes 5120
  71.5 25.2 %leaf.1 = (f32[512,512]{1,0:T(8,128)}, f32[4,128,128]{2,1,0:T(8,128)}) custom-call(s32[640]{0:T(1024)} %all-reduce.meta_ref, bf16[8,4,2,128,128]{4,3,2,1,0:T(8,128)(2,1)} %copy-done), custom_call_target="tpu_custom_call" | custom-call | tf_op jit(solution)/shard_map/leaf/pallas_call | solution.py:230
  96.7 0.0 all-to-all-done.1.in2_ref
  96.7 0.0 copy-start.9
  96.7 12.3 %panel.1 = (f32[512,512]{1,0:T(8,128)}, bf16[10,128,128]{2,1,0:T(8,128)(2,1)}) custom-call(s32[640]{0:T(1024)} %all-reduce.meta_ref, bf16[8,4,2,128,128]{4,3,2,1,0:T(8,128)(2,1)} %copy-done, bf16[8,4,2,128,128]{4,3,2,1,0:T(8,128)(2,1)} %all-to-all-done.1.in2_ref, f32[512,512]{1,0:T(8,128)} %get-tuple-element.14.l_ref, f32[4,128,128]{2,1,0:T(8,128)} %get-tuple-element.16.x_ref), custom_call_target="tpu_custom_call" | custom-call | tf_op jit(solution)/shard_map/panel/pallas_call | solution.py:283
  109.0 2.8 %collective-permute-start.2 = (bf16[10,128,128]{2,1,0:T(8,128)(2,1)}, bf16[10,128,128]{2,1,0:T(8,128)(2,1)S(1)}, u32[]{:S(2)}, u32[]{:S(2)}) collective-permute-start(bf16[10,128,128]{2,1,0:T(8,128)(2,1)} %get-tuple-element.18.a0), channel_id=1, source_target_pairs={{0,96},{8,104},{16,112},{24,120},{32,0},{40,8},{48,16},{56,24},{64... | collective-permute-start | bytes 983048 | tf_op jit(solution)/shard_map/ppermute | solution.py:356
  111.8 0.8 collective-permute-start.1
  112.5 0.9 collective-permute-start
  114.1 0.0 copy-done.9
  114.1 0.7 dynamic-slice.1
  114.8 0.7 bitcast_dynamic-update-slice_fusion
  115.5 17.3 %all-reduce.1.parent_ref = s32[16]{0:T(128)} all-reduce(s32[16]{0:T(128)S(1)} %bitcast_dynamic-update-slice_fusion), channel_id=2, replica_groups=mesh['col'=16,'blk'=8] {'col'}, use_global_device_ids=true, to_apply=%add.1 | all-reduce | flops 16 | bytes 128 | tf_op jit(solution)/shard_map/all_gather | solution.py:362
  132.8 0.0 collective-permute-done.2.a3
  132.8 0.0 copy-start.1
  132.8 0.0 collective-permute-done.1.a2
  132.8 0.0 collective-permute-done.a1
  132.8 0.7 copy-done.1
  133.5 0.1 copy-done.2
  133.6 0.7 copy-done.3
  134.3 3.0 %sort.1 = (f32[10,128,128]{2,1,0:T(8,128)}, bf16[10,128,128]{2,1,0:T(8,128)(2,1)}, bf16[10,128,128]{2,1,0:T(8,128)(2,1)}, bf16[10,128,128]{2,1,0:T(8,128)(2,1)}) custom-call(s32[16]{0:T(128)} %all-reduce.1.parent_ref, bf16[10,128,128]{2,1,0:T(8,128)(2,1)} %get-tuple-element.18.a0, bf16[10,128,128]{2,1,0:T(8,128)(2,1)} %copy-done.3, ...), custom_call_target="tpu_custom_call" | custom-call | tf_op jit(solution)/shard_map/sort/pallas_call | solution.py:320
  137.3 1.0 collective-permute-start.3
  138.4 1.3 collective-permute-start.4
  139.6 1.4 collective-permute-start.5
  141.0 11.8 %collective-permute-done.3.b1 = bf16[10,128,128]{2,1,0:T(8,128)(2,1)S(1)} collective-permute-done((bf16[10,128,128]{2,1,0:T(8,128)(2,1)}, bf16[10,128,128]{2,1,0:T(8,128)(2,1)S(1)}, u32[]{:S(2)}, u32[]{:S(2)}) %collective-permute-start.3) | collective-permute-done | bytes 327712 | tf_op jit(solution)/shard_map/ppermute | solution.py:356
  152.9 0.0 collective-permute-done.4.b2
  152.9 0.0 collective-permute-done.5.b3
  152.9 0.0 copy-start.6
  152.9 0.7 copy-done.4
  153.6 0.1 copy-done.5
  153.7 0.1 copy-done.6
  153.8 20.6 %parent.1 = f32[512,512]{1,0:T(8,128)} custom-call(f32[10,128,128]{2,1,0:T(8,128)} %get-tuple-element.19.keep_ref, bf16[10,128,128]{2,1,0:T(8,128)(2,1)} %copy-done.4, bf16[10,128,128]{2,1,0:T(8,128)(2,1)} %copy-done.5, bf16[10,128,128]{2,1,0:T(8,128)(2,1)} %copy-done.6), custom_call_target="tpu_custom_call" | custom-call | tf_op jit(solution)/shard_map/parent/pallas_call | solution.py:339
  (7 shorter events, 0.0 us)
Async XLA Ops:
  4.8 31.8 %all-to-all-start = ((bf16[8,4,2,128,128]{4,3,2,1,0:T(8,128)(2,1)}), bf16[8,4,2,128,128]{4,3,2,1,0:T(8,128)(2,1)S(1)}, u32[]{:S(2)}, u32[]{:S(2)}) async-start(bf16[8,4,2,128,128]{4,3,2,1,0:T(8,128)(2,1)} %place0.1), calls=%async_computation | async-start | bytes 4194304 | tf_op jit(solution)/shard_map/all_to_all | solution.py:365
  12.3 28.7 %copy-start.7 = (s32[16,4]{0,1:T(4,128)S(1)}, s32[16,4]{0,1:T(4,128)}, u32[]{:S(2)}) copy-start(s32[16,4]{0,1:T(4,128)} %param.7) | copy-start | bytes 772
  12.3 28.9 %copy-start.10 = (u32[128]{0:T(128)S(1)}, u32[128]{0:T(128)}, u32[]{:S(2)}) copy-start(u32[128]{0:T(128)} %constant.7) | copy-start | bytes 1540
  12.3 30.1 %copy-start.8 = (s32[16,1]{0,1:T(1,128)S(1)}, s32[16,1]{0,1:T(1,128)}, u32[]{:S(2)}) copy-start(s32[16,1]{0,1:T(1,128)} %param.8) | copy-start | bytes 196
  36.6 4.4 %copy-start = (bf16[8,4,2,128,128]{4,3,2,1,0:T(8,128)(2,1)}, bf16[8,4,2,128,128]{4,3,2,1,0:T(8,128)(2,1)S(1)}, u32[]{:S(2)}) copy-start(bf16[8,4,2,128,128]{4,3,2,1,0:T(8,128)(2,1)S(1)} %all-to-all-done.in_ref.in1_ref) | copy-start | bytes 6291460
  36.6 60.1 %all-to-all-start.1 = ((bf16[8,4,2,128,128]{4,3,2,1,0:T(8,128)(2,1)}), bf16[8,4,2,128,128]{4,3,2,1,0:T(8,128)(2,1)}, u32[]{:S(2)}, u32[]{:S(2)}) async-start(bf16[8,4,2,128,128]{4,3,2,1,0:T(8,128)(2,1)} %place1.1), calls=%async_computation.1 | async-start | bytes 4194304 | tf_op jit(solution)/shard_map/all_to_all | solution.py:365
  96.7 17.4 %copy-start.9 = (u32[128]{0:T(128)S(1)}, u32[128]{0:T(128)}, u32[]{:S(2)}) copy-start(u32[128]{0:T(128)} %constant.12) | copy-start | bytes 1540
  109.0 23.8 %collective-permute-start.2 = (bf16[10,128,128]{2,1,0:T(8,128)(2,1)}, bf16[10,128,128]{2,1,0:T(8,128)(2,1)S(1)}, u32[]{:S(2)}, u32[]{:S(2)}) collective-permute-start(bf16[10,128,128]{2,1,0:T(8,128)(2,1)} %get-tuple-element.18.a0), channel_id=1, source_target_pairs={{0,96},{8,104},{16,112},{24,120},{32,0},{40,8},{48,16},{56,24},{64... | collective-permute-start | bytes 983048 | tf_op jit(solution)/shard_map/ppermute | solution.py:356
  111.8 21.0 %collective-permute-start.1 = (bf16[10,128,128]{2,1,0:T(8,128)(2,1)}, bf16[10,128,128]{2,1,0:T(8,128)(2,1)S(1)}, u32[]{:S(2)}, u32[]{:S(2)}) collective-permute-start(bf16[10,128,128]{2,1,0:T(8,128)(2,1)} %get-tuple-element.18.a0), channel_id=1, source_target_pairs={{0,64},{8,72},{16,80},{24,88},{32,96},{40,104},{48,112},{56,120},{... | collective-permute-start | bytes 983048 | tf_op jit(solution)/shard_map/ppermute | solution.py:356
  112.5 20.2 %collective-permute-start = (bf16[10,128,128]{2,1,0:T(8,128)(2,1)}, bf16[10,128,128]{2,1,0:T(8,128)(2,1)S(1)}, u32[]{:S(2)}, u32[]{:S(2)}) collective-permute-start(bf16[10,128,128]{2,1,0:T(8,128)(2,1)} %get-tuple-element.18.a0), channel_id=1, source_target_pairs={{0,32},{8,40},{16,48},{24,56},{32,64},{40,72},{48,80},{56,88},{64,... | collective-permute-start | bytes 983048 | tf_op jit(solution)/shard_map/ppermute | solution.py:356
  132.8 0.7 copy-start.1
  132.8 0.8 copy-start.2
  133.6 0.7 copy-start.3
  137.3 15.5 %collective-permute-start.3 = (bf16[10,128,128]{2,1,0:T(8,128)(2,1)}, bf16[10,128,128]{2,1,0:T(8,128)(2,1)S(1)}, u32[]{:S(2)}, u32[]{:S(2)}) collective-permute-start(bf16[10,128,128]{2,1,0:T(8,128)(2,1)} %get-tuple-element.20), channel_id=1, source_target_pairs={{0,8},{8,16},{16,24},{24,0},{32,40},{40,48},{48,56},{56,32},{64,72... | collective-permute-start | bytes 983048 | tf_op jit(solution)/shard_map/ppermute | solution.py:356
  138.4 14.5 %collective-permute-start.4 = (bf16[10,128,128]{2,1,0:T(8,128)(2,1)}, bf16[10,128,128]{2,1,0:T(8,128)(2,1)S(1)}, u32[]{:S(2)}, u32[]{:S(2)}) collective-permute-start(bf16[10,128,128]{2,1,0:T(8,128)(2,1)} %get-tuple-element.21), channel_id=1, source_target_pairs={{0,16},{8,24},{16,0},{24,8},{32,48},{40,56},{48,32},{56,40},{64,80... | collective-permute-start | bytes 983048 | tf_op jit(solution)/shard_map/ppermute | solution.py:356
  139.6 13.2 %collective-permute-start.5 = (bf16[10,128,128]{2,1,0:T(8,128)(2,1)}, bf16[10,128,128]{2,1,0:T(8,128)(2,1)S(1)}, u32[]{:S(2)}, u32[]{:S(2)}) collective-permute-start(bf16[10,128,128]{2,1,0:T(8,128)(2,1)} %get-tuple-element.22), channel_id=1, source_target_pairs={{0,24},{8,0},{16,8},{24,16},{32,56},{40,32},{48,40},{56,48},{64,88... | collective-permute-start | bytes 983048 | tf_op jit(solution)/shard_map/ppermute | solution.py:356
  152.9 0.7 copy-start.4
  152.9 0.9 copy-start.5
  152.9 0.9 copy-start.6
